TPU v7x, 512 devices: a whole 4x8x8 slice. The times are simulated.
512 devices in a mesh: dp: 64 (over y, x, core), mp: 8 (over z).
Axes of the slice: x: 4, y: 8, z: 8, core: 2. Of those that a mesh axis runs over, the one named last changes fastest.
Arguments:
- partial_grads: bfloat16 [64, 2, 2, 512, 4096], P('dp', None, None, None, 'mp')
- factors: bfloat16 [8, 8, 512, 1024], P('mp', None, 'dp'), as said below
- inverse_factors: bfloat16 [8, 8, 512, 1024], P('mp', None, 'dp'), as said below
- probes: bfloat16 [8, 8, 512, 512], P('mp', None, 'dp'), may hold values from -6 to 6
- slot_table: int32 [8, 4], P('mp'), may hold values from 0 to 7, as said below
Outputs:
- preconditioned: bfloat16 [2, 2, 512, 4096], P(None, None, 'dp', 'mp')
- new_factors: bfloat16 [8, 8, 512, 1024], P('mp', None, 'dp')
Inputs may be any that keep to these rules, and one draw needn't show every extreme that they name: `slot_table`: in each row the 4 entries are distinct slots; slot j belongs to owner j // 2 (an owner is a group of 16 consecutive dp devices; the starting program sends slots 2k and 2k+1 to dp device 16k for updating), and in every row some owner holds 2 blocks. `factors`: both halves of every slot are upper triangular with a positive diagonal. `inverse_factors`: both halves of every slot are upper triangular with a positive diagonal.
All inputs are finite; a program needn't handle non-finite values. Where the computation divides by a largest or mean magnitude, that divisor is 1e-20 or more.
Results may differ from a plain program's by a relative error of at most 0.011.
Values may be sent and summed in bfloat16 or wider, within the bound.
A program may use at most 64 MiB of HBM per device.

v0:
```python
import math
import jax
import jax.numpy as jnp
import numpy as np
from jax import lax
from jax.sharding import PartitionSpec as P

GROUP = 16
CLIP_RMS = 0.3
LEARN_RATE = 0.1
EPS_NORM = 1e-06


def product(left_op, right_op):
    return jnp.dot(left_op, right_op, preferred_element_type=jnp.float32)


def step_factor(factor, first_gram, second_gram):
    bound_value = jnp.max(jnp.abs(first_gram + second_gram)) + EPS_NORM
    change = jnp.triu(first_gram - second_gram).astype(jnp.bfloat16)
    moved_rows = product(change, factor)
    return (factor.astype(jnp.float32) - LEARN_RATE / bound_value * moved_rows).astype(jnp.bfloat16)


def update_block(gradient, left_q, right_q, left_inv, right_inv, probe_mat):
    left_times = product(left_q, gradient).astype(jnp.bfloat16)
    whitened = product(left_times, right_q.T).astype(jnp.bfloat16)
    half_conjugate = product(left_inv.T, probe_mat).astype(jnp.bfloat16)
    conjugate = product(half_conjugate, right_inv).astype(jnp.bfloat16)
    new_left = step_factor(left_q, product(whitened, whitened.T), product(conjugate, conjugate.T))
    new_right = step_factor(right_q, product(whitened.T, whitened), product(conjugate.T, conjugate))
    precond_left = product(new_left.T, new_left).astype(jnp.bfloat16)
    precond_right = product(new_right.T, new_right).astype(jnp.bfloat16)
    middle = product(precond_left, gradient).astype(jnp.bfloat16)
    result = product(middle, precond_right).astype(jnp.bfloat16)
    return (result, jnp.concatenate([new_left, new_right], axis=1))


def pick_slots(onehot, source):
    return jnp.einsum("bj,jrc->brc", onehot, source, preferred_element_type=jnp.float32).astype(
        jnp.bfloat16
    )


def place_slots(onehot, source):
    return jnp.einsum("bj,brc->jrc", onehot, source, preferred_element_type=jnp.float32).astype(
        jnp.bfloat16
    )


def body(partial_grads, factors, inverse_factors, probes, slot_table):
    devices = lax.axis_size("dp")
    my_index = lax.axis_index("dp")
    local_sum = partial_grads[0].astype(jnp.float32)
    experts, block_rows, block_size, columns = local_sum.shape
    summed = lax.psum_scatter(local_sum, "dp", scatter_dimension=2, tiled=True)
    rows_dev = summed.shape[2]
    blocks_col = experts * block_rows
    gradient = summed.reshape(blocks_col, rows_dev, columns)
    entry_count = blocks_col * block_size * columns * lax.axis_size("mp")
    squares = lax.psum(jnp.sum(gradient * gradient), ("dp", "mp"))
    clip_factor = jnp.minimum(1.0, CLIP_RMS * math.sqrt(entry_count) / jnp.sqrt(squares + EPS_NORM))
    clipped = (gradient * clip_factor).astype(jnp.bfloat16)
    old_state = factors[0]
    combined_state = jnp.concatenate([old_state, inverse_factors[0]], axis=2)
    probe_rows = probes[0]
    own_slots = old_state.shape[0]
    slot_row = slot_table[0]
    onehot = (slot_row[:, None] == jnp.arange(own_slots, dtype=jnp.int32)[None, :]).astype(
        jnp.bfloat16
    )
    occupied = jnp.sum(onehot.astype(jnp.float32), axis=0) > 0.5
    slots_dev = own_slots // (devices // GROUP)
    target = np.arange(own_slots) // slots_dev * GROUP
    position = np.arange(own_slots) % slots_dev
    unit_grad = place_slots(onehot, clipped)
    global_rows = my_index * rows_dev + jnp.arange(rows_dev, dtype=jnp.int32)
    diagonal = (jnp.arange(columns, dtype=jnp.int32)[None, :] == global_rows[:, None]).astype(
        jnp.bfloat16
    )
    filler = jnp.concatenate([diagonal, diagonal, diagonal, diagonal], axis=1)
    send_grad = (
        jnp.zeros((devices, slots_dev, rows_dev, columns), jnp.bfloat16)
        .at[target, position]
        .set(unit_grad)
    )
    send_state = (
        jnp.broadcast_to(filler, (devices, slots_dev, rows_dev, 4 * columns))
        .at[target, position]
        .set(combined_state)
    )
    send_probe = (
        jnp.zeros((devices, slots_dev, rows_dev, columns), jnp.bfloat16)
        .at[target, position]
        .set(probe_rows)
    )
    grad_in = lax.all_to_all(send_grad, "dp", split_axis=0, concat_axis=2, tiled=True)
    state_in = lax.all_to_all(send_state, "dp", split_axis=0, concat_axis=2, tiled=True)
    probe_in = lax.all_to_all(send_probe, "dp", split_axis=0, concat_axis=2, tiled=True)

    def run_one(item_set):
        state = item_set[1]
        return update_block(
            item_set[0],
            state[:, :block_size],
            state[:, block_size : 2 * block_size],
            state[:, 2 * block_size : 3 * block_size],
            state[:, 3 * block_size :],
            item_set[2],
        )

    result, moved_rows = lax.map(run_one, (grad_in[0], state_in[0], probe_in[0]))
    back_grad = lax.all_to_all(result[None], "dp", split_axis=2, concat_axis=0, tiled=True)
    back_state = lax.all_to_all(moved_rows[None], "dp", split_axis=2, concat_axis=0, tiled=True)
    unit_back = back_grad[target, position]
    state_back = back_state[target, position]
    precond = pick_slots(onehot, unit_back)
    new_state = jnp.where(occupied[:, None, None], state_back, old_state)
    return (precond.reshape(experts, block_rows, rows_dev, columns), new_state[None])


def solution(mesh):
    return jax.shard_map(
        body,
        mesh=mesh,
        in_specs=(
            P("dp", None, None, None, "mp"),
            P("mp", None, "dp", None),
            P("mp", None, "dp", None),
            P("mp", None, "dp", None),
            P("mp", None),
        ),
        out_specs=(P(None, None, "dp", "mp"), P("mp", None, "dp", None)),
        check_vma=False,
    )
```

profile of v0, /device:TPU:2, one launch (start us, length us, event | category | flops | bytes accessed | tf_op | source)
XLA Modules:
  0.0 513.9 jit_solution(15969105971914788014)
XLA Ops:
  7.2 1.1 broadcast.29.clone.1
  8.3 2.3 scatter_fusion.2
  10.6 10.7 %all-to-all-start.2 = ((bf16[64,2,8,512]{3,2,1,0:T(8,128)(2,1)}), bf16[64,2,8,512]{3,2,1,0:T(8,128)(2,1)S(1)}, u32[]{:S(2)}, u32[]{:S(2)}) async-start(bf16[64,2,8,512]{3,2,1,0:T(8,128)(2,1)} %scatter_fusion.2), calls=%async_computation.3 | async-start | bytes 2097152 | tf_op jit(solution)/shard_map/all_to_all | solution.py:99
  21.4 2.5 broadcast_in_dim.73
  23.8 2.3 scatter_fusion
  26.1 23.9 %all-to-all-done.2 = bf16[64,2,8,512]{3,2,1,0:T(8,128)(2,1)S(1)} async-done(((bf16[64,2,8,512]{3,2,1,0:T(8,128)(2,1)}), bf16[64,2,8,512]{3,2,1,0:T(8,128)(2,1)S(1)}, u32[]{:S(2)}, u32[]{:S(2)}) %all-to-all-start.2) | async-done | bytes 1048608 | tf_op jit(solution)/shard_map/all_to_all | solution.py:99
  50.0 5.8 %all-to-all-start = ((bf16[64,2,8,2048]{3,2,1,0:T(8,128)(2,1)}), bf16[64,2,8,2048]{3,2,1,0:T(8,128)(2,1)}, u32[]{:S(2)}, u32[]{:S(2)}) async-start(bf16[64,2,8,2048]{3,2,1,0:T(8,128)(2,1)} %scatter_fusion), calls=%async_computation | async-start | bytes 8388608 | tf_op jit(solution)/shard_map/all_to_all | solution.py:98
  55.9 2.5 bitcast_convert_fusion
  58.5 158.2 %reduce-scatter.2.cloned.1.call-done = f32[2,2,8,512]{3,2,1,0:T(8,128)} async-done(((f32[2,2,512,512]{3,2,1,0:T(8,128)}), f32[2,2,8,512]{3,2,1,0:T(8,128)}) %reduce-scatter.2.cloned.1.call-update) | async-done | bytes 65552 | tf_op jit(solution)/shard_map/reduce_scatter | solution.py:56
  216.7 1.5 multiply_reduce_fusion
  218.2 97.7 %psum.7 = f32[]{:T(128)} all-reduce(f32[]{:T(128)} %multiply_reduce_fusion), channel_id=1, replica_groups=mesh['dp'=64,'mp'=8] {'dp','mp'}, use_global_device_ids=true, to_apply=%region_2.0 | all-reduce | flops 1 | bytes 8 | tf_op jit(solution)/shard_map/psum | solution.py:61
  317.7 1.1 broadcast.29.clone
  318.8 2.0 scatter_fusion.1
  320.8 8.5 %all-to-all-start.1 = ((bf16[64,2,8,512]{3,2,1,0:T(8,128)(2,1)}), bf16[64,2,8,512]{3,2,1,0:T(8,128)(2,1)S(1)}, u32[]{:S(2)}, u32[]{:S(2)}) async-start(bf16[64,2,8,512]{3,2,1,0:T(8,128)(2,1)} %scatter_fusion.1), calls=%async_computation.2 | async-start | bytes 2097152 | tf_op jit(solution)/shard_map/all_to_all | solution.py:97
  329.4 4.7 copy_bitcast_fusion
  334.1 24.0 %all-to-all-done.1 = bf16[64,2,8,512]{3,2,1,0:T(8,128)(2,1)S(1)} async-done(((bf16[64,2,8,512]{3,2,1,0:T(8,128)(2,1)}), bf16[64,2,8,512]{3,2,1,0:T(8,128)(2,1)S(1)}, u32[]{:S(2)}, u32[]{:S(2)}) %all-to-all-start.1) | async-done | bytes 1048608 | tf_op jit(solution)/shard_map/all_to_all | solution.py:97
  359.2 48.4 %while.12 = (s32[]{:T(128)}, bf16[2,512,512]{2,1,0:T(8,128)(2,1)}, bf16[2,512,1024]{1,2,0:T(8,128)(2,1)}, bf16[2,512,2048]{2,1,0:T(8,128)(2,1)}, bf16[2,512,512]...) while((s32[]{:T(128)}, bf16[2,512,512]{2,1,0:T(8,128)(2,1)}, ...), condition=%wide.region_9.10_spmd, body=%wide.region_6.9_spmd.sunk | while | flops 3768058368 | bytes 53485872 | solution.py:112
  359.2 2.1 constant_dynamic-slice_fusion.2
  361.3 2.5 copy.74
  363.8 1.9 convolution_convert_fusion.13
  367.0 1.9 convolution_convert_fusion.14
  368.9 1.1 abs_reduce_fusion.5
  370.7 2.6 fusion.115
  373.8 1.1 abs_reduce_fusion.4
  375.7 1.8 fusion.113
  377.5 1.1 fusion.117
  379.1 1.5 convolution_convert_fusion.15
  380.6 2.8 fusion.116
  383.4 2.1 constant_dynamic-slice_fusion.2
  385.5 2.5 copy.74
  388.0 1.9 convolution_convert_fusion.13
  391.2 1.9 convolution_convert_fusion.14
  393.1 1.1 abs_reduce_fusion.5
  394.9 2.6 fusion.115
  398.0 1.1 abs_reduce_fusion.4
  399.9 1.8 fusion.113
  403.3 1.5 convolution_convert_fusion.15
  404.8 2.7 fusion.116
  407.6 3.3 copy.72
  410.9 5.6 %all-to-all-start.3 = ((bf16[1,2,512,512]{3,1,0,2:T(2,128)(2,1)}), bf16[1,2,512,512]{3,1,0,2:T(2,128)(2,1)S(1)}, u32[]{:S(2)}, u32[]{:S(2)}) async-start(bf16[1,2,512,512]{3,1,0,2:T(2,128)(2,1)} %bitcast.83), calls=%async_computation.4 | async-start | bytes 2097152 | tf_op jit(solution)/shard_map/all_to_all | solution.py:113
  416.5 6.3 %copy.50 = bf16[2,512,1024]{2,0,1:T(2,128)(2,1)} copy(bf16[2,512,1024]{1,2,0:T(8,128)(2,1)} %get-tuple-element.36) | data formatting | bytes 4194304 | tf_op jit(solution)/shard_map/while | solution.py:112
  422.8 22.5 %all-to-all-done.3 = bf16[1,2,512,512]{3,1,0,2:T(2,128)(2,1)S(1)} async-done(((bf16[1,2,512,512]{3,1,0,2:T(2,128)(2,1)}), bf16[1,2,512,512]{3,1,0,2:T(2,128)(2,1)S(1)}, u32[]{:S(2)}, u32[]{:S(2)}) %all-to-all-start.3) | async-done | bytes 1048608 | tf_op jit(solution)/shard_map/all_to_all | solution.py:113
  445.3 5.7 %all-to-all-start.4 = ((bf16[1,2,512,1024]{3,1,0,2:T(2,128)(2,1)}), bf16[1,2,512,1024]{3,1,0,2:T(2,128)(2,1)S(1)}, u32[]{:S(2)}, u32[]{:S(2)}) async-start(bf16[1,2,512,1024]{3,1,0,2:T(2,128)(2,1)} %bitcast.26), calls=%async_computation.5 | async-start | bytes 4194304 | tf_op jit(solution)/shard_map/all_to_all | solution.py:114
  451.1 1.3 copy.71
  452.3 1.8 gather_fusion
  455.0 47.3 %all-to-all-done.4 = bf16[1,2,512,1024]{3,1,0,2:T(2,128)(2,1)S(1)} async-done(((bf16[1,2,512,1024]{3,1,0,2:T(2,128)(2,1)}), bf16[1,2,512,1024]{3,1,0,2:T(2,128)(2,1)S(1)}, u32[]{:S(2)}, u32[]{:S(2)}) %all-to-all-start.4) | async-done | bytes 2097184 | tf_op jit(solution)/shard_map/all_to_all | solution.py:114
  502.2 1.9 copy.70
  504.2 2.2 gather_fusion.1
  (56 shorter events, 9.6 us)
Async XLA Ops:
  7.2 14.2 %copy-start.7 = (bf16[1,8,8,1024]{3,2,1,0:T(8,128)(2,1)S(1)}, bf16[1,8,8,1024]{3,2,1,0:T(8,128)(2,1)}, u32[]{:S(2)}) copy-start(bf16[1,8,8,1024]{3,2,1,0:T(8,128)(2,1)} %param.20) | copy-start | bytes 393220
  7.2 14.2 %copy-start.8 = (bf16[1,8,8,1024]{3,2,1,0:T(8,128)(2,1)S(1)}, bf16[1,8,8,1024]{3,2,1,0:T(8,128)(2,1)}, u32[]{:S(2)}) copy-start(bf16[1,8,8,1024]{3,2,1,0:T(8,128)(2,1)} %param.21) | copy-start | bytes 393220
  10.6 39.5 %all-to-all-start.2 = ((bf16[64,2,8,512]{3,2,1,0:T(8,128)(2,1)}), bf16[64,2,8,512]{3,2,1,0:T(8,128)(2,1)S(1)}, u32[]{:S(2)}, u32[]{:S(2)}) async-start(bf16[64,2,8,512]{3,2,1,0:T(8,128)(2,1)} %scatter_fusion.2), calls=%async_computation.3 | async-start | bytes 2097152 | tf_op jit(solution)/shard_map/all_to_all | solution.py:99
  21.4 2.5 copy-start.6
  26.1 29.8 %copy-start.1 = (bf16[1,2,2,512,512]{4,3,2,1,0:T(8,128)(2,1)S(1)}, bf16[1,2,2,512,512]{4,3,2,1,0:T(8,128)(2,1)}, u32[]{:S(2)}) copy-start(bf16[1,2,2,512,512]{4,3,2,1,0:T(8,128)(2,1)} %param.19) | copy-start | bytes 6291460
  50.0 270.8 %all-to-all-start = ((bf16[64,2,8,2048]{3,2,1,0:T(8,128)(2,1)}), bf16[64,2,8,2048]{3,2,1,0:T(8,128)(2,1)}, u32[]{:S(2)}, u32[]{:S(2)}) async-start(bf16[64,2,8,2048]{3,2,1,0:T(8,128)(2,1)} %scatter_fusion), calls=%async_computation | async-start | bytes 8388608 | tf_op jit(solution)/shard_map/all_to_all | solution.py:98
  55.9 160.8 %reduce-scatter.2.cloned.1.call-start = ((), (), s32[]{:S(2)}) async-start(), calls=%async_computation.6 | async-start | bytes 4259840 | tf_op jit(solution)/shard_map/reduce_scatter | solution.py:56
  58.5 258.9 %copy-start.9 = (s32[1,4]{1,0:T(1,128)S(1)}, s32[1,4]{1,0:T(1,128)}, u32[]{:S(2)}) copy-start(s32[1,4]{1,0:T(1,128)} %param.23) | copy-start | bytes 52
  320.8 37.3 %all-to-all-start.1 = ((bf16[64,2,8,512]{3,2,1,0:T(8,128)(2,1)}), bf16[64,2,8,512]{3,2,1,0:T(8,128)(2,1)S(1)}, u32[]{:S(2)}, u32[]{:S(2)}) async-start(bf16[64,2,8,512]{3,2,1,0:T(8,128)(2,1)} %scatter_fusion.1), calls=%async_computation.2 | async-start | bytes 2097152 | tf_op jit(solution)/shard_map/all_to_all | solution.py:97
  359.2 4.6 copy-start.2
  365.7 1.2 copy-start.4
  374.9 2.6 copy-start
  377.5 1.6 copy-start.5
  380.6 2.8 copy-start.3
  383.4 4.6 copy-start.2
  389.9 1.2 copy-start.4
  399.1 2.6 copy-start
  401.7 1.6 copy-start.5
  404.8 2.7 copy-start.3
  410.9 34.4 %all-to-all-start.3 = ((bf16[1,2,512,512]{3,1,0,2:T(2,128)(2,1)}), bf16[1,2,512,512]{3,1,0,2:T(2,128)(2,1)S(1)}, u32[]{:S(2)}, u32[]{:S(2)}) async-start(bf16[1,2,512,512]{3,1,0,2:T(2,128)(2,1)} %bitcast.83), calls=%async_computation.4 | async-start | bytes 2097152 | tf_op jit(solution)/shard_map/all_to_all | solution.py:113
  445.3 56.9 %all-to-all-start.4 = ((bf16[1,2,512,1024]{3,1,0,2:T(2,128)(2,1)}), bf16[1,2,512,1024]{3,1,0,2:T(2,128)(2,1)S(1)}, u32[]{:S(2)}, u32[]{:S(2)}) async-start(bf16[1,2,512,1024]{3,1,0,2:T(2,128)(2,1)} %bitcast.26), calls=%async_computation.5 | async-start | bytes 4194304 | tf_op jit(solution)/shard_map/all_to_all | solution.py:114
Sparse Core Ops, SparseCore 0:
  61.4 155.2 reduce-scatter.1
where the time goes:
time: 516 us; the launch traced here: 514 us
  waiting for transfers between devices  276 us (53%)
  blocking collectives  97.7 us (19%)
  local copies, waits for them, and re-layouts  46.2 us (9%)
  starting transfers between devices  36.3 us (7%)
  matrix products  31.9 us (6%)
  between operations  14.9 us (3%)
  other arithmetic  7.96 us (2%)
    reduce_scatter x1, waiting for transfers between devices, body(): summed = lax.psum_scatter(local_sum, 'dp', scatter_dimension=2, tiled=True)  158 us
    psum x1, blocking collectives, body(): squares = lax.psum(jnp.sum(gradient * gradient), ('dp', 'mp'))  97.7 us
    all_to_all x1, waiting for transfers between devices, body(): lax.all_to_all(moved_rows[None], 'dp', split_axis=2, concat_axis=0, tiled...  47.3 us
    dot_general x20, matrix products, product(): return jnp.dot(left_op, right_op, preferred_element_type=jnp.float32)  31.4 us
    all_to_all x1, waiting for transfers between devices, body(): lax.all_to_all(send_grad, 'dp', split_axis=0, concat_axis=2, tiled=True)  24 us
    all_to_all x1, waiting for transfers between devices, body(): lax.all_to_all(send_probe, 'dp', split_axis=0, concat_axis=2, tiled=True)  23.9 us
    all_to_all x1, waiting for transfers between devices, body(): lax.all_to_all(result[None], 'dp', split_axis=2, concat_axis=0, tiled=True)  22.5 us
    all_to_all x1, starting transfers between devices, body(): lax.all_to_all(send_probe, 'dp', split_axis=0, concat_axis=2, tiled=True)  10.7 us
  transfers between devices with their start and end apart: 6, of which 5 were waited for; matrix products, arithmetic and copies ran while one was open for 5% of the time, Pallas kernels for 0%

commit v1 on v0

--- a/solution.py
+++ b/solution.py
@@ -110,7 +110,10 @@
         )
 
     result, moved_rows = lax.map(run_one, (grad_in[0], state_in[0], probe_in[0]))
-    back_grad = lax.all_to_all(result[None], "dp", split_axis=2, concat_axis=0, tiled=True)
+    back_grad = jnp.concatenate(
+        lax.all_to_all(jnp.stack(jnp.split(result[None], lax.axis_size("dp"), axis=2)), "dp", 0, 0),
+        axis=0,
+    )
     back_state = lax.all_to_all(moved_rows[None], "dp", split_axis=2, concat_axis=0, tiled=True)
     unit_back = back_grad[target, position]
     state_back = back_state[target, position]

time: 516 us -> 601 us (1.16)
  local copies, waits for them, and re-layouts: 46.2 us -> 127 us
    unnamed x11 -> x74, local copies, waits for them, and re-layouts: 0.65 us -> 83.6 us
  transfers between devices with their start and end apart: 6 -> 6, of which waited for: 5 -> 5; matrix products, arithmetic and copies ran while one was open for 5% -> 4% of each run, Pallas kernels for 0% -> 0%
where the time goes in v1:
time: 601 us; the launch traced here: 596 us
  waiting for transfers between devices  278 us (46%)
  local copies, waits for them, and re-layouts  127 us (21%)
  blocking collectives  97.7 us (16%)
  starting transfers between devices  36.6 us (6%)
  matrix products  30.4 us (5%)
  between operations  14.9 us (2%)
  other arithmetic  7.93 us (1%)
    reduce_scatter x1, waiting for transfers between devices, body(): summed = lax.psum_scatter(local_sum, 'dp', scatter_dimension=2, tiled=True)  158 us
    psum x1, blocking collectives, body(): squares = lax.psum(jnp.sum(gradient * gradient), ('dp', 'mp'))  97.7 us
    unnamed x74, local copies, waits for them, and re-layouts  83.6 us
    all_to_all x1, waiting for transfers between devices, body(): lax.all_to_all(moved_rows[None], 'dp', split_axis=2, concat_axis=0, tiled...  49.8 us
    dot_general x20, matrix products, product(): return jnp.dot(left_op, right_op, preferred_element_type=jnp.float32)  29.9 us
    all_to_all x1, waiting for transfers between devices, body(): lax.all_to_all(send_grad, 'dp', split_axis=0, concat_axis=2, tiled=True)  24 us
    all_to_all x1, waiting for transfers between devices, body(): lax.all_to_all(send_probe, 'dp', split_axis=0, concat_axis=2, tiled=True)  23.9 us
    all_to_all x1, waiting for transfers between devices, body(): lax.all_to_all(jnp.stack(jnp.split(result[None], lax.axis_size('dp'), axi...  22.5 us
  transfers between devices with their start and end apart: 6, of which 5 were waited for; matrix products, arithmetic and copies ran while one was open for 4% of the time, Pallas kernels for 0%

profile of v1, /device:TPU:2, one launch (start us, length us, event | category | flops | bytes accessed | tf_op | source)
XLA Modules:
  0.0 595.6 jit_solution(7945940527080874917)
XLA Ops:
  8.3 2.3 scatter_fusion.2
  10.6 10.7 %all-to-all-start.2 = ((bf16[64,2,8,512]{3,2,1,0:T(8,128)(2,1)}), bf16[64,2,8,512]{3,2,1,0:T(8,128)(2,1)S(1)}, u32[]{:S(2)}, u32[]{:S(2)}) async-start(bf16[64,2,8,512]{3,2,1,0:T(8,128)(2,1)} %scatter_fusion.2), calls=%async_computation.3 | async-start | bytes 2097152 | tf_op jit(solution)/shard_map/all_to_all | solution.py:99
  21.4 2.5 broadcast_in_dim.73
  23.8 2.3 scatter_fusion
  26.1 23.9 %all-to-all-done.2 = bf16[64,2,8,512]{3,2,1,0:T(8,128)(2,1)S(1)} async-done(((bf16[64,2,8,512]{3,2,1,0:T(8,128)(2,1)}), bf16[64,2,8,512]{3,2,1,0:T(8,128)(2,1)S(1)}, u32[]{:S(2)}, u32[]{:S(2)}) %all-to-all-start.2) | async-done | bytes 1048608 | tf_op jit(solution)/shard_map/all_to_all | solution.py:99
  50.0 5.8 all-to-all-start
  55.9 2.5 bitcast_convert_fusion
  58.5 158.2 %reduce-scatter.2.cloned.1.call-done = f32[2,2,8,512]{3,2,1,0:T(8,128)} async-done(((f32[2,2,512,512]{3,2,1,0:T(8,128)}), f32[2,2,8,512]{3,2,1,0:T(8,128)}) %reduce-scatter.2.cloned.1.call-update) | async-done | bytes 65552 | tf_op jit(solution)/shard_map/reduce_scatter | solution.py:56
  216.7 1.5 multiply_reduce_fusion
  218.2 97.7 %psum.7 = f32[]{:T(128)} all-reduce(f32[]{:T(128)} %multiply_reduce_fusion), channel_id=1, replica_groups=mesh['dp'=64,'mp'=8] {'dp','mp'}, use_global_device_ids=true, to_apply=%region_2.0 | all-reduce | flops 1 | bytes 8 | tf_op jit(solution)/shard_map/psum | solution.py:61
  318.8 2.0 scatter_fusion.1
  320.8 8.5 %all-to-all-start.1 = ((bf16[64,2,8,512]{3,2,1,0:T(8,128)(2,1)}), bf16[64,2,8,512]{3,2,1,0:T(8,128)(2,1)S(1)}, u32[]{:S(2)}, u32[]{:S(2)}) async-start(bf16[64,2,8,512]{3,2,1,0:T(8,128)(2,1)} %scatter_fusion.1), calls=%async_computation.2 | async-start | bytes 2097152 | tf_op jit(solution)/shard_map/all_to_all | solution.py:97
  329.4 4.7 copy_bitcast_fusion
  334.1 24.0 %all-to-all-done.1 = bf16[64,2,8,512]{3,2,1,0:T(8,128)(2,1)S(1)} async-done(((bf16[64,2,8,512]{3,2,1,0:T(8,128)(2,1)}), bf16[64,2,8,512]{3,2,1,0:T(8,128)(2,1)S(1)}, u32[]{:S(2)}, u32[]{:S(2)}) %all-to-all-start.1) | async-done | bytes 1048608 | tf_op jit(solution)/shard_map/all_to_all | solution.py:97
  359.2 48.8 %while.12 = (s32[]{:T(128)}, bf16[2,512,512]{2,1,0:T(8,128)(2,1)}, bf16[2,512,1024]{1,2,0:T(8,128)(2,1)}, bf16[2,512,2048]{2,1,0:T(8,128)(2,1)}, bf16[2,512,512]...) while((s32[]{:T(128)}, bf16[2,512,512]{2,1,0:T(8,128)(2,1)}, ...), condition=%wide.region_9.10_spmd, body=%wide.region_6.9_spmd.sunk | while | flops 3768058368 | bytes 61874028 | solution.py:112
  359.2 2.1 constant_dynamic-slice_fusion.2
  361.3 2.5 copy.65
  363.8 1.9 convolution_convert_fusion.13
  367.0 1.9 convolution_convert_fusion.14
  370.7 2.6 fusion.115
  375.7 1.8 fusion.113
  379.1 1.6 convolution_convert_fusion.15
  380.7 1.9 fusion.116
  383.6 2.1 constant_dynamic-slice_fusion.2
  385.7 2.5 copy.65
  388.3 1.9 convolution_convert_fusion.13
  391.4 1.9 convolution_convert_fusion.14
  395.2 2.6 fusion.115
  400.1 1.8 fusion.113
  403.6 1.6 convolution_convert_fusion.15
  405.1 1.9 fusion.116
  415.9 1.3 constant_dynamic-update-slice_fusion.57
  419.9 1.3 constant_dynamic-update-slice_fusion.54
  426.5 1.3 constant_dynamic-update-slice_fusion.49
  441.0 1.3 constant_dynamic-update-slice_fusion.38
  446.2 1.3 constant_dynamic-update-slice_fusion.34
  451.5 1.3 constant_dynamic-update-slice_fusion.30
  456.8 1.3 constant_dynamic-update-slice_fusion.26
  467.3 1.3 constant_dynamic-update-slice_fusion.18
  477.8 1.3 constant_dynamic-update-slice_fusion.10
  479.2 1.3 constant_dynamic-update-slice_fusion.9
  492.3 5.9 all-to-all-start.3
  498.2 6.3 %copy.47 = bf16[2,512,1024]{2,0,1:T(2,128)(2,1)} copy(bf16[2,512,1024]{1,2,0:T(8,128)(2,1)} %get-tuple-element.36) | data formatting | bytes 4194304 | tf_op jit(solution)/shard_map/while | solution.py:112
  504.5 22.5 %all-to-all-done.3 = bf16[64,1,2,8,512]{4,3,2,1,0:T(8,128)(2,1)S(1)} async-done(((bf16[64,1,2,8,512]{4,3,2,1,0:T(8,128)(2,1)}), bf16[64,1,2,8,512]{4,3,2,1,0:T(8,128)(2,1)S(1)}, u32[]{:S(2)}, u32[]{:S(2)}) %all-to-all-start.3) | async-done | bytes 1048608 | tf_op jit(solution)/shard_map/all_to_all | solution.py:114
  527.0 5.7 all-to-all-start.4
  534.2 49.8 %all-to-all-done.4 = bf16[1,2,512,1024]{3,1,0,2:T(2,128)(2,1)S(1)} async-done(((bf16[1,2,512,1024]{3,1,0,2:T(2,128)(2,1)}), bf16[1,2,512,1024]{3,1,0,2:T(2,128)(2,1)S(1)}, u32[]{:S(2)}, u32[]{:S(2)}) %all-to-all-start.4) | async-done | bytes 2097184 | tf_op jit(solution)/shard_map/all_to_all | solution.py:117
  583.9 1.9 copy.63
  585.9 2.2 gather_fusion.1
  (126 shorter events, 91.0 us)
Async XLA Ops:
  7.2 14.2 %copy-start.9 = (bf16[1,8,8,1024]{3,2,1,0:T(8,128)(2,1)S(1)}, bf16[1,8,8,1024]{3,2,1,0:T(8,128)(2,1)}, u32[]{:S(2)}) copy-start(bf16[1,8,8,1024]{3,2,1,0:T(8,128)(2,1)} %param.20) | copy-start | bytes 393220
  7.2 14.2 %copy-start.10 = (bf16[1,8,8,1024]{3,2,1,0:T(8,128)(2,1)S(1)}, bf16[1,8,8,1024]{3,2,1,0:T(8,128)(2,1)}, u32[]{:S(2)}) copy-start(bf16[1,8,8,1024]{3,2,1,0:T(8,128)(2,1)} %param.21) | copy-start | bytes 393220
  10.6 39.5 %all-to-all-start.2 = ((bf16[64,2,8,512]{3,2,1,0:T(8,128)(2,1)}), bf16[64,2,8,512]{3,2,1,0:T(8,128)(2,1)S(1)}, u32[]{:S(2)}, u32[]{:S(2)}) async-start(bf16[64,2,8,512]{3,2,1,0:T(8,128)(2,1)} %scatter_fusion.2), calls=%async_computation.3 | async-start | bytes 2097152 | tf_op jit(solution)/shard_map/all_to_all | solution.py:99
  21.4 2.5 copy-start.8
  26.1 29.8 %copy-start.1 = (bf16[1,2,2,512,512]{4,3,2,1,0:T(8,128)(2,1)S(1)}, bf16[1,2,2,512,512]{4,3,2,1,0:T(8,128)(2,1)}, u32[]{:S(2)}) copy-start(bf16[1,2,2,512,512]{4,3,2,1,0:T(8,128)(2,1)} %param.19) | copy-start | bytes 6291460
  50.0 270.8 %all-to-all-start = ((bf16[64,2,8,2048]{3,2,1,0:T(8,128)(2,1)}), bf16[64,2,8,2048]{3,2,1,0:T(8,128)(2,1)}, u32[]{:S(2)}, u32[]{:S(2)}) async-start(bf16[64,2,8,2048]{3,2,1,0:T(8,128)(2,1)} %scatter_fusion), calls=%async_computation | async-start | bytes 8388608 | tf_op jit(solution)/shard_map/all_to_all | solution.py:98
  55.9 160.8 %reduce-scatter.2.cloned.1.call-start = ((), (), s32[]{:S(2)}) async-start(), calls=%async_computation.6 | async-start | bytes 4259840 | tf_op jit(solution)/shard_map/reduce_scatter | solution.py:56
  58.5 258.9 %copy-start.11 = (s32[1,4]{1,0:T(1,128)S(1)}, s32[1,4]{1,0:T(1,128)}, u32[]{:S(2)}) copy-start(s32[1,4]{1,0:T(1,128)} %param.23) | copy-start | bytes 52
  320.8 37.3 %all-to-all-start.1 = ((bf16[64,2,8,512]{3,2,1,0:T(8,128)(2,1)}), bf16[64,2,8,512]{3,2,1,0:T(8,128)(2,1)S(1)}, u32[]{:S(2)}, u32[]{:S(2)}) async-start(bf16[64,2,8,512]{3,2,1,0:T(8,128)(2,1)} %scatter_fusion.1), calls=%async_computation.2 | async-start | bytes 2097152 | tf_op jit(solution)/shard_map/all_to_all | solution.py:97
  359.2 4.6 copy-start.4
  365.7 1.2 copy-start.6
  375.0 2.6 copy-start
  377.5 1.6 copy-start.7
  377.5 3.2 copy-start.2
  380.7 2.9 copy-start.5
  382.6 1.0 copy-start.3
  383.6 4.6 copy-start.4
  390.2 1.2 copy-start.6
  399.4 2.6 copy-start
  401.9 1.6 copy-start.7
  402.0 3.2 copy-start.2
  405.1 2.9 copy-start.5
  407.1 1.0 copy-start.3
  492.3 34.7 %all-to-all-start.3 = ((bf16[64,1,2,8,512]{4,3,2,1,0:T(8,128)(2,1)}), bf16[64,1,2,8,512]{4,3,2,1,0:T(8,128)(2,1)S(1)}, u32[]{:S(2)}, u32[]{:S(2)}) async-start(bf16[64,1,2,8,512]{4,3,2,1,0:T(8,128)(2,1)} %constant_dynamic-update-slice_fusion), calls=%async_computation.4 | async-start | bytes 2097152 | tf_op jit(solution)/shard_map/all_to_all | solution.py:114
  527.0 56.9 %all-to-all-start.4 = ((bf16[1,2,512,1024]{3,1,0,2:T(2,128)(2,1)}), bf16[1,2,512,1024]{3,1,0,2:T(2,128)(2,1)S(1)}, u32[]{:S(2)}, u32[]{:S(2)}) async-start(bf16[1,2,512,1024]{3,1,0,2:T(2,128)(2,1)} %bitcast.88), calls=%async_computation.5 | async-start | bytes 4194304 | tf_op jit(solution)/shard_map/all_to_all | solution.py:117
Sparse Core Ops, SparseCore 0:
  61.4 155.2 reduce-scatter.1
